TPU v7x, 128 devices: a whole 4x4x4 slice. The times are simulated.
128 devices in a mesh: slab: 32 (over z, x, y_lo), sec: 4 (over y_hi, core).
Axes of the slice: x: 4, y: 4 (y_hi: 2, y_lo: 2; y = y_hi * 2 + y_lo), z: 4, core: 2. Of those that a mesh axis runs over, the one named last changes fastest.
Arguments:
- fixed_image: float32 [2560, 80, 640], P('slab', 'sec'), may hold values from -16 to 16
- moving_image: float32 [2560, 80, 640], P('slab', 'sec'), may hold values from -16 to 16
- lattice_fine: float32 [3, 128, 5, 33], P(None, 'slab'), may hold values from -4 to 4
- lattice_mid: float32 [3, 33, 2, 9], replicated, may hold values from -4 to 4
- lattice_coarse: float32 [3, 9, 1, 3], replicated, may hold values from -4 to 4
- offset_fine: int32 [3, 128, 4], P(None, 'slab'), may hold values from -4 to 3
- offset_mid: int32 [3, 32, 1], P(None, 'slab'), may hold values from -4 to 3
- offset_coarse: int32 [3, 8, 1], replicated, may hold values from -4 to 3
Outputs:
- fine_step: float32 [3, 128, 5, 33], P(None, 'slab')
- mid_step: float32 [3, 33, 2, 9], replicated
- coarse_step: float32 [3, 9, 1, 3], replicated
All inputs are finite; a program needn't handle non-finite values.
Results may differ from a plain program's by a relative error of at most 0.0003.
Values sent between devices are 32-bit elements; how exact they have to be, the bound alone decides.
A program may use at most 320 MiB of HBM per device.

v0:
```python
import functools

import jax
import jax.numpy as jnp
import ml_dtypes
import numpy as np
from jax import lax
from jax.experimental import pallas as pl
from jax.experimental.pallas import tpu as pltpu
from jax.sharding import PartitionSpec as P

SP = 20
EPSILON = 1e-06
STEP_SIZE = 0.5
HIGHEST = lax.Precision.HIGHEST
F32 = jnp.float32
BF16 = jnp.bfloat16
MESH = pl.DeviceIdType.MESH
SLABS = 32
SECS = 4
NZ, NY, NX = 80, 20, 640
CHUNKS = NX // 128
LOG2E = 1.4426950408889634
VMEM_LIMIT = 58 * 1024 * 1024


def basis(rows, knots, factor, coarse):
    rows, knots = np.asarray(rows, np.float64), np.asarray(knots, np.float64)
    position = factor * rows + 0.5 * (factor - 1)
    centre = SP * coarse * knots + 0.5 * (coarse - 1)
    distance = np.abs((position[:, None] - centre[None, :]) / (SP * coarse))
    near = 2.0 / 3.0 - distance**2 + 0.5 * distance**3
    far = np.maximum(2.0 - distance, 0.0) ** 3 / 6.0
    return np.where(distance < 1.0, near, far)


def two_parts(values):
    high = values.astype(ml_dtypes.bfloat16)
    low = (values - high.astype(np.float64)).astype(ml_dtypes.bfloat16)
    return high, low


def right_parts(values):
    high, low = two_parts(values)
    return np.concatenate([high, low, high], axis=-2)


def wide_parts(values):
    high, low = two_parts(values)
    zero = np.zeros_like(high)
    return np.concatenate([np.concatenate([high, low], 1), np.concatenate([high, zero], 1)], 0)


def one_hot(condition):
    return condition.astype(ml_dtypes.bfloat16)


@functools.cache
def tables():
    t = {}
    rz, ry = np.zeros((4, 4, 24, 64)), np.zeros((4, NY, 64))
    z, y, x = np.arange(NZ), np.arange(NY), np.arange(NX)
    for r in range(4):
        for block in range(4):
            rows = z[20 * block : 20 * block + 20]
            for a in range(7):
                rz[r, block, :20, a:40:8] = basis(rows, [a - 1], 1, 1)
            for a in range(5):
                rz[r, block, :20, 40 + a : 56 : 8] = basis(rows, [a - 2], 1, 4)
                rz[r, block, :20, 56 + a : 57 + a] = basis(rows + 80 * r, [a - 2], 1, 16)
    for s in range(4):
        for a in range(7):
            ry[s, :, a:40:8] = basis(y + 20 * s, range(5), 1, 1)
        for a in range(5):
            ry[s, :, 40 + a : 56 : 8] = basis(y + 20 * s, range(2), 1, 4)
            ry[s, :, 56 + a : 57 + a] = basis(y + 20 * s, [0], 1, 16)
    whole = rz[:, None, :, None] * ry[None, :, None, :, None, :]
    high, low = two_parts(whole.reshape(16, 1920, 64))
    t["spread"] = np.concatenate([high, low, high, low], axis=2)
    t["gather"] = np.concatenate([high[:4, :, :40], low[:4, :, :40]], axis=2).transpose(0, 2, 1)
    across = np.zeros((3, 128, NX))
    across[0, :33] = basis(x, range(33), 1, 1).T
    across[1, :9] = basis(x, range(9), 1, 4).T
    across[2, :3] = basis(x, range(3), 1, 16).T
    t["bt"] = right_parts(-LOG2E * across)
    along = np.zeros((3, NX, 128))
    for d in range(3):
        along[d, :, 40 * d : 40 * d + 33] = basis(x, range(33), 1, 1)
    t["bx"] = np.concatenate([wide_parts(along[d]) for d in range(3)], axis=0)
    rz, ry = np.zeros((4, 24, 32)), np.zeros((4, 5, 32))
    z, y, x = np.arange(20), np.arange(5), np.arange(160)
    for r in range(4):
        for a in range(4):
            rz[r, :20, a:16:8] = basis(z, [a - 1], 4, 4)
        for a in range(5):
            rz[r, :20, 16 + a : 17 + a] = basis(z + 20 * r, [a - 2], 4, 16)
    for s in range(4):
        for a in range(4):
            ry[s, :, a:16:8] = basis(y + 5 * s, range(2), 4, 4)
        for a in range(5):
            ry[s, :, 16 + a : 17 + a] = basis(y + 5 * s, [0], 4, 16)
    whole = np.zeros((16, 128, 32))
    whole[:, :120] = (rz[:, None, None] * ry[None, :, :, None]).reshape(16, 120, 32)
    high, low = two_parts(whole)
    t["mspread"] = np.concatenate([high, high, low, np.zeros_like(low)], axis=2)
    t["mgather"] = np.concatenate([high[:, :, :16], low[:, :, :16]], axis=2).transpose(0, 2, 1)
    across = np.zeros((2, 128, 256))
    across[0, :9, :160] = basis(x, range(9), 4, 4).T
    across[1, :3, :160] = basis(x, range(3), 4, 16).T
    t["mbt"] = right_parts(-LOG2E * across)
    along = np.zeros((3, 256, 128))
    for d in range(3):
        along[d, :160, 16 * d : 16 * d + 9] = basis(x, range(9), 4, 4)
    t["mbx"] = wide_parts(along.reshape(768, 128))
    rz = np.zeros((4, 8, 32))
    z, y, x = np.arange(5), np.arange(5), np.arange(40)
    for r in range(4):
        for a in range(4):
            rz[r, :5, a : a + 1] = basis(z + 5 * r, [a - 1], 16, 16)
    whole = np.zeros((4, 128, 32))
    whole[:, :40] = (rz[:, None] * basis(y, [0], 16, 16)[None, :, None]).reshape(4, 40, 32)
    high, low = two_parts(whole)
    t["cspread"] = np.concatenate([high, high, low, np.zeros_like(low)], axis=2)
    t["cgather"] = np.concatenate([high[:, :, :16], low[:, :, :16]], axis=2).transpose(0, 2, 1)
    across = np.zeros((128, 128))
    across[:3, :40] = basis(x, range(3), 16, 16).T
    t["cbt"] = right_parts(-LOG2E * across)
    along = np.zeros((3, 128, 128))
    for d in range(3):
        along[d, :40, 16 * d : 16 * d + 3] = basis(x, range(3), 16, 16)
    t["cbx"] = wide_parts(along.reshape(384, 128))
    row, column = np.arange(NX)[:, None], np.arange(256)[None, :]
    t["px"] = one_hot(row // 4 == column)
    row, column = np.arange(120)[:, None], np.arange(400)[None, :]
    t["pz"] = one_hot((row // 24 == column // 80) & (row % 24 == column % 80 // 4))
    row, column = np.arange(512)[:, None], np.arange(128)[None, :]
    t["pcx"] = one_hot((row % 256 < 160) & (row // 256 * 64 + row % 256 // 4 == column))
    row, column = np.arange(16)[:, None], np.arange(48)[None, :]
    t["pcz"] = one_hot((row // 8 == column // 24) & (column % 24 < 20) & (row % 8 == column % 24 // 4))
    row, column, place = np.arange(16)[:, None], np.arange(128)[None, :], np.arange(32)[:, None, None]
    knot = place - 1 - row // 8 + row % 8
    t["rows_m"] = one_hot((knot == column) & (column < 33))
    t["rows_c"] = one_hot((knot == column) & (column < 9))[:8]
    row, column, place = np.arange(24)[:, None], np.arange(256)[None, :], np.arange(8)[:, None, None]
    knot = np.where(row < 16, row - 2, row - 16 + place - 2)
    found = (knot == column // 32 - 1 + column % 8) & (column % 8 < 4) & (knot >= 0) & (knot < 9)
    t["sum_c"] = one_hot(found)
    row, column, place = np.arange(112)[:, None], np.arange(512)[None, :], np.arange(32)[:, None, None]
    knot = np.where(row < 96, row % 48 - 2, row % 8 + place - 2)
    b = np.where(row < 96, row // 48, (row - 96) // 8)
    found = (knot == column // 16 - 1 + column % 8) & (column % 8 < 4) & (column // 8 % 2 == b)
    t["sum_m"] = one_hot(found & (knot >= 0) & (knot < 33))
    return t


def dot(a, b):
    return jnp.dot(a, b, preferred_element_type=F32)


def dot_rows(a, b):
    return lax.dot_general(
        a, b, (((0,), (0,)), ((), ())), precision=HIGHEST, preferred_element_type=F32
    )


def parts(values):
    high = values.astype(BF16)
    return high, (values - high.astype(F32)).astype(BF16)


def dot3(a, right):
    high, low = parts(a)
    return dot(jnp.concatenate([high, high, low], axis=1), right)


def dot_wide(a, table):
    wide = dot(jnp.concatenate(parts(a), axis=1), table)
    return wide[:, 0:128] + wide[:, 128:256]


def dot_exact(table, b):
    wide = dot(table, jnp.concatenate(parts(b), axis=1))
    return wide[:, 0:128] + wide[:, 128:256]


def dot_gather(table, b):
    n = table.shape[0] // 2
    wide = dot(table, jnp.concatenate(parts(b), axis=1))
    return (wide[0:n, 0:128] + wide[0:n, 128:256]) + wide[n:, 0:128]


def stacked(column, n):
    high, low = parts(jnp.concatenate([column, jnp.zeros((32 - n, column.shape[1]), F32)], axis=0))
    return jnp.concatenate([high, low, high, jnp.zeros_like(low)], axis=0)


def from_lane(values, lane):
    return values if lane == 0 else pltpu.roll(values, 128 - lane, 1)


def shift_lanes(chunks, shift):
    amount = (128 - shift) & 127
    rolled = [pltpu.roll(chunk, amount, 1) for chunk in chunks]
    lane = lax.broadcasted_iota(jnp.int32, chunks[0].shape, 1)
    first = lane < jnp.maximum(-shift, 0)
    last = lane >= 128 - jnp.maximum(shift, 0)
    zero = jnp.zeros_like(chunks[0])
    padded = [zero, *rolled, zero]
    return [
        jnp.where(first, padded[j], jnp.where(last, padded[j + 2], padded[j + 1]))
        for j in range(len(chunks))
    ]


def fraction(exponent):
    grown = jnp.exp2(exponent)
    frac = pl.reciprocal(1.0 + grown, approx=True)
    return frac, frac * (grown * frac)


def weights(fixed, corner, step, fractions):
    (fz, gz), (fy, gy), (fx, gx) = fractions
    line = [[corner[z][y] + fx * step[z][y] for y in (0, 1)] for z in (0, 1)]
    rise = [line[z][1] - line[z][0] for z in (0, 1)]
    plane = [line[z][0] + fy * rise[z] for z in (0, 1)]
    slope_z = plane[1] - plane[0]
    residual = (plane[0] + fz * slope_z) - fixed
    slope_y = rise[0] + fz * (rise[1] - rise[0])
    along = [step[z][0] + fy * (step[z][1] - step[z][0]) for z in (0, 1)]
    slope_x = along[0] + fz * (along[1] - along[0])
    return [
        (residual * slope_z) * gz,
        (residual * slope_y) * gy,
        (residual * slope_x) * gx,
    ]


def greet(k, s):
    barrier = pltpu.get_barrier_semaphore()

    def signal(slab, sec):
        pl.semaphore_signal(barrier, inc=1, device_id=(slab, sec), device_id_type=MESH)

    @pl.loop(1, SLABS)
    def _(i):
        signal((k + i) & (SLABS - 1), s)

    for i in range(1, SECS):
        other = (s + i) & (SECS - 1)
        signal(k, other)
        signal((k + 1) & (SLABS - 1), other)
        signal((k + SLABS - 1) & (SLABS - 1), other)
    return lambda: pl.semaphore_wait(barrier, SLABS - 1 + 3 * (SECS - 1))


def broadcast_start(k, s, tile, buffer, send_sem, recv_sem):
    @pl.loop(0, SLABS - 1)
    def _(i):
        pltpu.make_async_remote_copy(
            src_ref=tile,
            dst_ref=buffer.at[k],
            send_sem=send_sem,
            recv_sem=recv_sem,
            device_id=((k + 16 + i + (i > 15).astype(jnp.int32)) & (SLABS - 1), s),
            device_id_type=MESH,
        ).start()


def broadcast_wait(buffer, send_sem, recv_sem):
    part = buffer.at[pl.ds(0, SLABS - 1)]
    pltpu.make_async_copy(part, part, recv_sem).wait()
    pltpu.make_async_copy(part, part, send_sem).wait()


def remote(src, dst, send_sem, recv_sem, device):
    return pltpu.make_async_remote_copy(
        src_ref=src,
        dst_ref=dst,
        send_sem=send_sem,
        recv_sem=recv_sem,
        device_id=device,
        device_id_type=MESH,
    )


def around(k, s, source, buffer, send, recv, act):
    slabs = ((k + SLABS - 1) & (SLABS - 1), k, (k + 1) & (SLABS - 1))

    def one(dk, other):
        if act == "wait_recv":
            copy = remote(source, buffer.at[dk, other], send.at[dk, other], recv.at[dk, other], (k, other))
        else:
            copy = remote(
                source, buffer.at[2 - dk, s], send.at[dk, other], recv.at[2 - dk, s], (slabs[dk], other)
            )
        getattr(copy, act)()

    for dk in (0, 2):
        for other in range(SECS):
            one(dk, other)
    for i in range(1, SECS):
        one(1, (s + i) & (SECS - 1))


TABLES = {
    "px": None, "pz": None, "pcx": None, "pcz": None,
    "rows_m": "k", "rows_c": "q", "cspread": "r", "cgather": "r", "cbt": None, "cbx": None,
    "sum_c": "q", "mspread": "rs", "mgather": "rs", "mbt": None, "mbx": None,
    "spread": "rs", "gather": "s", "bt": None, "bx": None, "sum_m": "k",
}


def finish(result, fine_out, mid_out, coarse_out):
    for d in range(3):
        for b in range(5):
            row = 40 * d + 8 * b
            fine_out[d, b] = result[row : row + 4, 0:33]
        for a in range(9):
            for b in range(2):
                row = 120 + 48 * b + 16 * d + a
                mid_out[d, a, b : b + 1, :] = result[row : row + 1, 0:33]
        for a in range(3):
            row = 216 + 16 * d + a
            coarse_out[d, a] = result[row : row + 1, 0:9]


def kernel(
    moving, fixed, lat_fine, lat_mid, lat_coarse, off_fine, off_mid, off_coarse, *refs
):
    n = len(TABLES)
    stored, refs = refs[:n], refs[n:]
    result, *refs = refs
    t = dict(zip(TABLES, refs[:n]))
    (
        pad, fx, sums, zlo, zhi, z_bef, z_aft, y_bef, y_aft, corners,
        lf_own, lf_up, lf_down, lf_prev, lf_next, lf, mt, ct,
        pooled_m, pooled_f, pack_up, pack_down, pm_bef, pm_aft, pm_halo, pm_same,
        piece, pieces, cv, cf, mm,
        c_tile, c_buf, m_part, m_parts, m_tile, m_buf,
        at, by, columns, field_a, field_b, split_a, split_b, adjoint, mixed,
        f_part, f_parts, f_tile, f_buf,
        load_sem, table_sem, send, recv, psend, precv, fsend, frecv, tsend, trecv, bsem,
    ) = refs[n:]
    k, s = lax.axis_index("slab"), lax.axis_index("sec")
    nxt, prv = (k + 1) & (SLABS - 1), (k + SLABS - 1) & (SLABS - 1)
    q, r = k >> 2, k & 3
    has_prev, has_next = (k > 0).astype(F32), (k < SLABS - 1).astype(F32)
    up, down = s < SECS - 1, s > 0
    own_y, own_z = pl.ds(4, NY), pl.ds(8, NZ)

    load_moving = [
        pltpu.make_async_copy(
            moving.at[:, :, pl.ds(128 * c, 128)], pad.at[c, own_y, own_z], load_sem.at[c]
        )
        for c in range(CHUNKS)
    ]
    load_fixed = [
        pltpu.make_async_copy(
            fixed.at[:, :, pl.ds(128 * c, 128)], fx.at[c, :, pl.ds(0, NZ)], load_sem.at[CHUNKS + c]
        )
        for c in range(CHUNKS)
    ]
    place = {"k": k, "q": q, "r": r, "s": s, "rs": 4 * r + s}
    load_table = {}
    for i, (name, which) in enumerate(TABLES.items()):
        source = stored[i] if which is None else stored[i].at[place[which]]
        load_table[name] = pltpu.make_async_copy(source, t[name], table_sem.at[i])
    for copy in load_moving:
        copy.start()
    all_here = greet(k, s)
    for copy in (*load_fixed, *load_table.values()):
        copy.start()

    def table(name):
        load_table[name].wait()
        return t[name]

    lat_to_next = remote(lf_up, lf_prev, send.at[0], recv.at[0], (nxt, s))
    lat_to_prev = remote(lf_down, lf_next, send.at[1], recv.at[1], (prv, s))
    z_to_next = remote(zhi, z_bef, send.at[2], recv.at[2], (nxt, s))
    z_to_prev = remote(zlo, z_aft, send.at[3], recv.at[3], (prv, s))
    to_bef = remote(moving.at[pl.ds(16, 4)], y_bef, send.at[4], recv.at[4], (k, s + 1))
    to_aft = remote(moving.at[pl.ds(0, 4)], y_aft, send.at[5], recv.at[5], (k, s - 1))
    first, last = pl.ds(0, 2), pl.ds(8, 2)
    corner_up = [
        remote(zhi.at[:, last], corners.at[0], send.at[6], recv.at[6], (nxt, s + 1)),
        remote(zlo.at[:, last], corners.at[1], send.at[7], recv.at[7], (prv, s + 1)),
    ]
    corner_down = [
        remote(zhi.at[:, first], corners.at[2], send.at[8], recv.at[8], (nxt, s - 1)),
        remote(zlo.at[:, first], corners.at[3], send.at[9], recv.at[9], (prv, s - 1)),
    ]
    head, tail = pl.ds(0, 8), pl.ds(16, 8)
    mid_same = [
        remote(pooled_m.at[:, tail], pm_same.at[0], send.at[10], recv.at[10], (nxt, s)),
        remote(pooled_m.at[:, head], pm_same.at[1], send.at[11], recv.at[11], (prv, s)),
    ]
    mid_up = [
        remote(pack_up, pm_bef, send.at[12], recv.at[12], (k, s + 1)),
        remote(pack_up.at[:, tail], pm_halo.at[0, 0], send.at[13], recv.at[13], (nxt, s + 1)),
        remote(pack_up.at[:, head], pm_halo.at[1, 0], send.at[14], recv.at[14], (prv, s + 1)),
    ]
    mid_down = [
        remote(pack_down, pm_aft, send.at[15], recv.at[15], (k, s - 1)),
        remote(pack_down.at[:, tail], pm_halo.at[0, 1], send.at[16], recv.at[16], (nxt, s - 1)),
        remote(pack_down.at[:, head], pm_halo.at[1, 1], send.at[17], recv.at[17], (prv, s - 1)),
    ]

    def start_y_halos(*parts_of_z):
        rows = [pl.ds(16 * part, 16) for part in parts_of_z]

        @pl.when(up)
        def _():
            for z in rows:
                remote(moving.at[pl.ds(16, 4), z], y_bef.at[:, z], send.at[4], recv.at[4], (k, s + 1)).start()

        @pl.when(down)
        def _():
            for z in rows:
                remote(moving.at[pl.ds(0, 4), z], y_aft.at[:, z], send.at[5], recv.at[5], (k, s - 1)).start()

    def start(*copies):
        for copy in copies:
            copy.start()

    def start_if(condition, *copies):
        @pl.when(condition)
        def _():
            start(*copies)

    for c in range(CHUNKS):
        pad[c, :, 0:8, :] = jnp.zeros((28, 8, 128), F32)
        pad[c, :, 88:96, :] = jnp.zeros((28, 8, 128), F32)
        fx[c, :, 80:88, :] = jnp.zeros((NY, 8, 128), F32)
        for block in range(4):
            at[block, c, :, 24:32, :] = jnp.zeros((21, 8, 128), F32)
            by[block, c, :, 24:32, :] = jnp.zeros((21, 8, 128), F32)
    all_here()
    start_y_halos(0, 1)
    for c in range(CHUNKS):
        load_moving[c].wait()

        @pl.loop(0, NY // 2, unroll=5)
        def _(pair):
            for half in range(2):
                rows = slice(4 * half, 4 * half + 4)
                zlo[c, pair, rows, :] = pad[c, 2 * pair + half + 4, 8:12, :]
                zhi[c, pair, rows, :] = pad[c, 2 * pair + half + 4, 84:88, :]

    start(z_to_next)

    px, pz = table("px"), table("pz")

    def pooled():
        high, low = parts(sums[...].reshape(400, NX))
        high, low = parts(dot(high, px[...]) + dot(low, px[...]))
        return ((dot(pz[...], high) + dot(pz[...], low)) * (1.0 / 64.0)).reshape(5, 24, 256)

    for c in range(CHUNKS):
        lanes = slice(128 * c, 128 * c + 128)

        @pl.loop(0, 5, unroll=5)
        def _(group):
            four = [pad[c, 4 * group + 4 + i, 8:88, :] for i in range(4)]
            sums[group, :, lanes] = (four[0] + four[1]) + (four[2] + four[3])

    pooled_m[...] = pooled()

    for c in range(CHUNKS):
        load_fixed[c].wait()
        lanes = slice(128 * c, 128 * c + 128)

        @pl.loop(0, 5, unroll=5)
        def _(group):
            four = [fx[c, 4 * group + i, 0:80, :] for i in range(4)]
            sums[group, :, lanes] = (four[0] + four[1]) + (four[2] + four[3])

    pooled_f[...] = pooled()

    halves = []
    for ref in (pooled_m, pooled_f):
        upper, lower = jnp.zeros((24, 256), F32), jnp.zeros((24, 256), F32)
        for i in range(5):
            keep = (i + s < 4).astype(F32)
            upper = upper + ref[i] * keep
            lower = lower + ref[i] * (1.0 - keep)
        halves.append(jnp.concatenate([upper, lower], axis=0))
    high, low = parts(jnp.concatenate(halves, axis=1))
    pcx, pcz = table("pcx")[...], table("pcz")[...]
    both = dot(high, pcx) + dot(low, pcx)
    piece[...] = (dot_exact(pcz, both) * (1.0 / 64.0)).reshape(2, 8, 128)
    around(k, s, piece, pieces, psend, precv, "start")
    pieces[1, s] = piece[...]
    for ref, first_y in ((pack_up, 1), (pack_down, 0)):
        ref[0:4] = pooled_m[first_y : first_y + 4, :, 0:128]
        others = [pooled_m[first_y + i, :, 128:256] for i in range(4)]
        ref[4] = (others[0] + pltpu.roll(others[1], 32, 1)) + (
            pltpu.roll(others[2], 64, 1) + pltpu.roll(others[3], 96, 1)
        )
    start(*mid_same)
    start_if(up, *mid_up)
    start_if(down, *mid_down)

    for ref in (lf_own, mt, ct, cv, mm):
        ref[...] = jnp.zeros_like(ref)
    for d in range(3):
        for b in range(5):
            lf_own[d, b, 0:4, 0:33] = lat_fine[d, b]
        for a in range(9):
            for b in range(2):
                row = 32 * d + 16 * b + a
                mt[row : row + 1, 0:33] = lat_mid[d, a, b : b + 1]
        for a in range(3):
            ct[16 * d + a : 16 * d + a + 1, 0:9] = lat_coarse[d, a]
    for d in range(3):
        for b in range(5):
            row = 5 * d + b
            lf_up[row : row + 1, :] = lf_own[d, b, 3:4, :]
            lf_down[2 * row : 2 * row + 2, :] = lf_own[d, b, 0:2, :]
    start(lat_to_next, lat_to_prev)

    def pick_rows(name, ref):
        rows = table(name)[...]
        contract = (((1,), (1,)), ((), ()))
        high, low = parts(ref[...])
        return lax.dot_general(rows, high, contract, preferred_element_type=F32) + lax.dot_general(
            rows, low, contract, preferred_element_type=F32
        )

    rows_m, rows_c = pick_rows("rows_m", mt), pick_rows("rows_c", ct)
    cbt, cspread = table("cbt")[...], table("cspread")[...]
    column = dot3(jnp.concatenate([from_lane(rows_c[0:8], 16 * d) for d in range(3)], axis=0), cbt)
    column = jnp.concatenate([column[8 * d : 8 * d + 8] for d in range(3)], axis=1)
    exponent = dot(cspread, stacked(column, 8))[0:40]
    fractions_c = [fraction(exponent[:, 128 * d : 128 * d + 128]) for d in range(3)]
    cbx, cgather = table("cbx"), table("cgather")

    around(k, s, piece, pieces, psend, precv, "wait_recv")

    lane = lax.broadcasted_iota(jnp.int32, (5, 128), 1)
    for dk in range(3):
        scale = (has_prev, jnp.float32(1.0), has_next)[dk]
        rows = (slice(3, 8), slice(8, 13), slice(13, 18))[dk]
        for c in range(5):
            value = jnp.zeros((8, 128), F32)
            if c < 4:
                value = value + pieces[dk, c, 0]
            if c > 0:
                value = value + pieces[dk, c - 1, 1]
            cv[4 + c, rows, :] = jnp.where(lane < 40, value[0:5], 0.0) * scale
            if dk == 1:
                cf[c] = value
    fixed_c = pltpu.roll(cf[...].reshape(40, 128), 64, 1)

    oz, oy, ox = off_coarse[0, 0, q], off_coarse[1, 0, q], off_coarse[2, 0, q]
    a_z, b_z = [], []
    for e in (0, 1):
        window = cv[pl.ds(4 + oy, 6), pl.ds(8 + oz + e, 8), :].reshape(48, 128)
        here, there = shift_lanes([window], ox)[0], shift_lanes([window], ox + 1)[0]
        a_z.append(here)
        b_z.append(there - here)
    corner = [[a_z[z][8 * y : 8 * y + 40] for y in (0, 1)] for z in (0, 1)]
    step = [[b_z[z][8 * y : 8 * y + 40] for y in (0, 1)] for z in (0, 1)]
    total = jnp.concatenate(weights(fixed_c, corner, step, fractions_c), axis=1)
    total = dot_wide(jnp.concatenate([total, jnp.zeros((8, 384), F32)], axis=0), cbx[...])
    total = jnp.concatenate([total, jnp.zeros((80, 128), F32)], axis=0)
    c_tile[...] = dot_gather(cgather[...], total)[0:8]
    broadcast_start(k, s, c_tile, c_buf, bsem.at[0], bsem.at[1])
    c_buf[k] = c_tile[...]
    start_y_halos(2, 3)
    start(z_to_prev)

    mbt, mspread, mbx, mgather = table("mbt"), table("mspread"), table("mbx"), table("mgather")
    own = [from_lane(rows_m[0:8], 32 * d + 16 * b) for d in range(3) for b in range(2)]
    own = dot3(jnp.concatenate(own, axis=0), mbt[0])
    coarse = dot3(jnp.concatenate([from_lane(rows_c[8:16], 16 * d) for d in range(3)], axis=0), mbt[1])
    column = [
        jnp.concatenate([own[16 * d : 16 * d + 16], coarse[8 * d : 8 * d + 8]], axis=0) for d in range(3)
    ]
    base_m = dot(mspread[...], stacked(jnp.concatenate(column, axis=1), 24))[0:120]
    sum_c = table("sum_c")

    @pl.when(s == 0)
    def _():
        y_bef[...] = jnp.zeros_like(y_bef)
        corners[0:2] = jnp.zeros((2, CHUNKS, 2, 8, 128), F32)
        pm_bef[...] = jnp.zeros_like(pm_bef)
        pm_halo[:, 0] = jnp.zeros((2, 5, 8, 128), F32)

    @pl.when(s == SECS - 1)
    def _():
        y_aft[...] = jnp.zeros_like(y_aft)
        corners[2:4] = jnp.zeros((2, CHUNKS, 2, 8, 128), F32)
        pm_aft[...] = jnp.zeros_like(pm_aft)
        pm_halo[:, 1] = jnp.zeros((2, 5, 8, 128), F32)

    for copy in mid_same:
        copy.wait_recv()

    @pl.when(s > 0)
    def _():
        for copy in mid_up:
            copy.wait_recv()

    @pl.when(s < SECS - 1)
    def _():
        for copy in mid_down:
            copy.wait_recv()

    for c in range(2):
        lanes = slice(128 * c, 128 * c + 128)
        for y in range(5):
            mm[c, 5 + y, 4:8, :] = pm_same[0, y, 0:4, lanes] * has_prev
            mm[c, 5 + y, 8:28, :] = pooled_m[y, 0:20, lanes]
            mm[c, 5 + y, 28:32, :] = pm_same[1, y, 0:4, lanes] * has_next
    few = lax.broadcasted_iota(jnp.int32, (24, 128), 1) < 32
    for e, (whole, first_y) in enumerate(((pm_bef, 1), (pm_aft, 10))):
        for y in range(4):
            for c in range(2):

                def row(ref):
                    value = ref[y] if c == 0 else from_lane(ref[4], 32 * y)
                    return value if c == 0 else jnp.where(few[0 : value.shape[0]], value, 0.0)

                mm[c, first_y + y, 4:8, :] = row(pm_halo.at[0, e])[0:4] * has_prev
                mm[c, first_y + y, 8:28, :] = row(whole)[0:20]
                mm[c, first_y + y, 28:32, :] = row(pm_halo.at[1, e])[0:4] * has_next

    oz, oy, ox = off_mid[0, 0, 0], off_mid[0, 0, 1], off_mid[0, 0, 2]
    a_z, b_z = [], []
    for e in (0, 1):
        window = [mm[c, pl.ds(5 + oy, 6), pl.ds(8 + oz + e, 24), :].reshape(144, 128) for c in range(2)]
        here, there = shift_lanes(window, ox), shift_lanes(window, ox + 1)
        a_z.append(here)
        b_z.append([there[c] - here[c] for c in range(2)])

    def make_window(block, oz, oy, ox, y):
        window = [pad[c, 4 + oy + y, pl.ds(20 * block + 8 + oz, 24), :] for c in range(CHUNKS)]
        here, there = shift_lanes(window, ox), shift_lanes(window, ox + 1)
        for c in range(CHUNKS):
            at[block, c, y, 0:24, :] = here[c]
            by[block, c, y, 0:24, :] = there[c] - here[c]

    def make_windows(blocks, ranges):
        @pl.loop(*blocks)
        def _(block):
            offsets = [off_fine[d, block, s] for d in range(3)]
            for first_y, last_y, unroll in ranges:
                pl.loop(first_y, last_y, unroll=unroll)(functools.partial(make_window, block, *offsets))

    broadcast_wait(c_buf, bsem.at[0], bsem.at[1])
    gradient = dot_exact(sum_c[...], c_buf[...].reshape(256, 128))
    near_c = gradient[16:24]
    gradient = gradient[0:16]
    inverse = lax.rsqrt(jnp.sum(gradient * gradient) * (1.0 / 81.0) + EPSILON)

    near = dot3(jnp.concatenate([from_lane(near_c, 16 * d) for d in range(3)], axis=0), mbt[1])
    near = jnp.concatenate([near[8 * d : 8 * d + 8] for d in range(3)], axis=1)
    near = dot(mspread[...], stacked(jnp.concatenate([jnp.zeros((16, 768), F32), near], axis=0), 24))
    exponent = base_m - (STEP_SIZE * inverse) * near[0:120]
    fixed_m = pooled_f[...].reshape(120, 256)
    found = []
    for c in range(2):
        lanes = slice(128 * c, 128 * c + 128)
        corner = [[a_z[z][c][24 * y : 24 * y + 120] for y in (0, 1)] for z in (0, 1)]
        step = [[b_z[z][c][24 * y : 24 * y + 120] for y in (0, 1)] for z in (0, 1)]
        fractions = [fraction(exponent[:, 256 * d + 128 * c : 256 * d + 128 * c + 128]) for d in range(3)]
        found.append(weights(fixed_m[:, lanes], corner, step, fractions))
    total = jnp.concatenate([found[c][d] for d in range(3) for c in range(2)], axis=1)
    total = dot_wide(jnp.concatenate([total, jnp.zeros((8, 768), F32)], axis=0), mbx[...])
    m_part[...] = dot_gather(mgather[...], total)

    def part_copies(act):
        for i in range(1, SECS):
            other = (s + i) & (SECS - 1)
            slot = other if act == "wait_recv" else s
            getattr(remote(m_part, m_parts.at[slot], tsend.at[other], trecv.at[slot], (k, other)), act)()

    part_copies("start")
    start_y_halos(4)
    start_if(up, *corner_up)
    start_if(down, *corner_down)
    m_parts[s] = m_part[...]

    gradient = gradient * inverse
    next_c = [
        from_lane(rows_c[8:16], 16 * d) - (STEP_SIZE * inverse) * from_lane(near_c, 16 * d) for d in range(3)
    ]
    for copy in (lat_to_next, lat_to_prev):
        copy.wait_recv()
    for d in range(3):
        for b in range(5):
            lf[d, 8 * b : 8 * b + 1, :] = lf_prev[5 * d + b : 5 * d + b + 1, :] * has_prev
            lf[d, 8 * b + 1 : 8 * b + 5, :] = lf_own[d, b, 0:4, :]
            lf[d, 8 * b + 5 : 8 * b + 7, :] = lf_next[10 * d + 2 * b : 10 * d + 2 * b + 2, :] * has_next
            lf[d, 8 * b + 7 : 8 * b + 8, :] = jnp.zeros((1, 128), F32)
    bt = table("bt")
    own = dot3(lf[...].reshape(120, 128), bt[0])
    mid = [from_lane(rows_m[8:16], 32 * d + 16 * b) for d in range(3) for b in range(2)]
    mid = dot3(jnp.concatenate(mid, axis=0), bt[1])
    coarse = dot3(jnp.concatenate(next_c, axis=0), bt[2])
    base_f = [
        jnp.concatenate(
            [own[40 * d : 40 * d + 40], mid[16 * d : 16 * d + 16], coarse[8 * d : 8 * d + 8]], axis=0
        )
        for d in range(3)
    ]
    base_f = jnp.concatenate(base_f, axis=1)

    make_windows((1, 3), ((4, 16, 3),))
    part_copies("wait_recv")
    m_tile[...] = (m_parts[0] + m_parts[1]) + (m_parts[2] + m_parts[3])
    broadcast_start(k, s, m_tile, m_buf, bsem.at[2], bsem.at[3])
    m_buf[k] = m_tile[...]

    turn_r = lax.broadcasted_iota(jnp.int32, (48, 128), 0)
    turn = jnp.where(turn_r == lax.broadcasted_iota(jnp.int32, (48, 128), 1) + 2, 1.0, 0.0)
    result[216:264, :] = dot_rows(gradient, turn[0:16])[0:48]

    for copy in (z_to_next, z_to_prev):
        copy.wait_recv()

    @pl.when(s > 0)
    def _():
        for copy in (to_bef, *corner_up):
            copy.wait_recv()

    @pl.when(s < SECS - 1)
    def _():
        for copy in (to_aft, *corner_down):
            copy.wait_recv()

    for c in range(CHUNKS):
        lanes = slice(128 * c, 128 * c + 128)
        pad[c, 0:4, 8:88, :] = y_bef[:, :, lanes]
        pad[c, 24:28, 8:88, :] = y_aft[:, :, lanes]

    @pl.loop(0, NY // 2, unroll=2)
    def _(pair):
        for half in range(2):
            rows = slice(4 * half, 4 * half + 4)
            for c in range(CHUNKS):
                pad[c, 2 * pair + half + 4, 4:8, :] = z_bef[c, pair, rows, :] * has_prev
                pad[c, 2 * pair + half + 4, 88:92, :] = z_aft[c, pair, rows, :] * has_next

    for y in range(4):
        rows = slice(4 * (y % 2), 4 * (y % 2) + 4)
        for c in range(CHUNKS):
            for n in range(2):
                where = slice(4, 8) if n == 0 else slice(88, 92)
                keep = has_prev if n == 0 else has_next
                pad[c, y, where, :] = corners[n, c, y // 2, rows, :] * keep
                pad[c, 24 + y, where, :] = corners[2 + n, c, y // 2, rows, :] * keep

    make_windows((1, 3), ((0, 4, 2), (16, 21, 5)))
    make_windows((0, 1), ((0, 21, 3),))
    make_windows((3, 4), ((0, 21, 3),))

    spread, gather, bx, sum_m = table("spread"), table("gather"), table("bx"), table("sum_m")

    broadcast_wait(m_buf, bsem.at[2], bsem.at[3])
    gradient = dot_exact(sum_m[...], m_buf[...].reshape(512, 128))
    near = gradient[96:112]
    gradient = gradient[0:96]
    inverse = lax.rsqrt(jnp.sum(gradient * gradient) * (1.0 / 1782.0) + EPSILON)

    near = dot3(jnp.concatenate([from_lane(near, 16 * d) for d in range(3)], axis=0), bt[1])
    near = jnp.concatenate([near[16 * d : 16 * d + 16] for d in range(3)], axis=1)
    near = jnp.concatenate([jnp.zeros((40, 3 * NX), F32), near, jnp.zeros((8, 3 * NX), F32)], axis=0)
    upper, lower = parts(base_f - (STEP_SIZE * inverse) * near)
    columns[0:64, :] = upper
    columns[64:128, :] = upper
    columns[128:192, :] = lower
    columns[192:256, :] = lower
    field_a[...] = dot(spread[0:480, :], columns[...])

    rows_z = (pl.ds(0, 24), pl.ds(jnp.minimum(k + 1, 1), 24))

    def fine_block(block, split, split_before, field, field_after):
        adjoint[...] = jnp.zeros_like(adjoint)
        after = pl.ds(pl.multiple_of(480 * jnp.minimum(block + 1, 3), 480), 480)

        @pl.loop(0, 5)
        def _(i):
            lanes = pl.ds(pl.multiple_of(384 * i, 384), 384)
            field_after[:, lanes] = dot(spread[after, :], columns[:, lanes])
            lanes = pl.ds(pl.multiple_of(768 * i, 768), 768)
            adjoint[...] += dot(split_before[:, lanes], bx[lanes, :])
            for pair in range(2):
                for c in range(CHUNKS):
                    found = []
                    for h in range(2):
                        y = 4 * i + 2 * pair + h
                        corner = [[at[block, c, y + e, z, :] for e in (0, 1)] for z in rows_z]
                        step = [[by[block, c, y + e, z, :] for e in (0, 1)] for z in rows_z]
                        rows = pl.ds(pl.multiple_of(24 * y, 8), 24)
                        fractions = [
                            fraction(field[rows, NX * d + 128 * c : NX * d + 128 * c + 128]) for d in range(3)
                        ]
                        atlas = fx[c, y, pl.ds(20 * block, 24), :]
                        found.append(weights(atlas, corner, step, fractions))
                    rows = pl.ds(pl.multiple_of(96 * i + 48 * pair, 48), 48)
                    for d in range(3):
                        upper, lower = parts(jnp.concatenate([found[0][d], found[1][d]], axis=0))
                        lane = 2 * NX * d + 128 * c
                        split[rows, lane : lane + 128] = upper
                        split[rows, lane + NX : lane + NX + 128] = lower

        before = pl.ds(pl.multiple_of(480 * jnp.maximum(block - 1, 0), 480), 480)
        mixed[before, :] = adjoint[:, 0:128] + adjoint[:, 128:256]

    @pl.loop(0, 2)
    def _(two):
        fine_block(2 * two, split_a, split_b, field_a, field_b)
        fine_block(2 * two + 1, split_b, split_a, field_b, field_a)

    wide = dot(split_b[...], bx[...])
    mixed[1440:1920, :] = wide[:, 0:128] + wide[:, 128:256]
    f_part[...] = dot_gather(gather[...], mixed[...])
    around(k, s, f_part, f_parts, fsend, frecv, "start")
    f_parts[1, s] = f_part[...]

    for b in range(2):
        turned = dot_rows(gradient[48 * b : 48 * b + 48] * inverse, turn)
        result[120 + 48 * b : 168 + 48 * b, :] = turned[0:48]
    row = lax.broadcasted_iota(jnp.int32, (40, 128), 0) & 7

    around(k, s, f_part, f_parts, fsend, frecv, "wait_recv")
    before, middle, after = ((f_parts[i, 0] + f_parts[i, 1]) + (f_parts[i, 2] + f_parts[i, 3]) for i in range(3))
    middle = middle + jnp.where((row == 1) | (row == 2), pltpu.roll(before * has_prev, 36, 0), 0.0)
    middle = middle + jnp.where(row == 4, pltpu.roll(after * has_next, 4, 0), 0.0)
    middle = jnp.where((row >= 1) & (row <= 4), middle, 0.0)
    f_tile[...] = jnp.full((8, 128), jnp.sum(middle * middle))
    broadcast_start(k, s, f_tile, f_buf, bsem.at[4], bsem.at[5])
    f_buf[k] = f_tile[...]

    for copy in (lat_to_next, lat_to_prev, z_to_next, z_to_prev, *mid_same):
        copy.wait_send()

    @pl.when(up)
    def _():
        for copy in (to_bef, *corner_up, *mid_up):
            copy.wait_send()

    @pl.when(down)
    def _():
        for copy in (to_aft, *corner_down, *mid_down):
            copy.wait_send()

    around(k, s, piece, pieces, psend, precv, "wait_send")
    around(k, s, f_part, f_parts, fsend, frecv, "wait_send")
    part_copies("wait_send")
    middle = pltpu.roll(middle, 39, 0)
    thirds = [from_lane(middle, 40 * d) for d in range(3)]

    broadcast_wait(f_buf, bsem.at[4], bsem.at[5])
    squares = jnp.sum(f_buf[...], axis=0)[0:1, :]
    inverse = lax.rsqrt(squares * (1.0 / 63360.0) + EPSILON)
    for d in range(3):
        result[40 * d : 40 * d + 40, :] = thirds[d] * inverse


def body(
    fixed_image,
    moving_image,
    lattice_fine,
    lattice_mid,
    lattice_coarse,
    offset_fine,
    offset_mid,
    offset_coarse,
):
    t = tables()
    vmem, smem, hbm = (pl.BlockSpec(memory_space=m) for m in (pltpu.VMEM, pltpu.SMEM, pl.ANY))
    shape = lambda *dims: jax.ShapeDtypeStruct(dims, F32)
    buf = lambda *dims: pltpu.VMEM(dims, F32)
    half = lambda *dims: pltpu.VMEM(dims, BF16)
    dma = lambda *dims: pltpu.SemaphoreType.DMA(dims)
    result = pl.pallas_call(
        kernel,
        out_shape=shape(264, 128),
        in_specs=[hbm, hbm, vmem, vmem, vmem, smem, smem, smem] + [hbm] * len(TABLES),
        out_specs=vmem,
        scratch_shapes=[
            *[pltpu.VMEM(t[n].shape[which is not None :], t[n].dtype) for n, which in TABLES.items()],
            buf(CHUNKS, 28, 96, 128), buf(CHUNKS, NY, 88, 128), buf(5, NZ, NX),
            *[buf(CHUNKS, 10, 8, 128)] * 4, *[buf(4, NZ, NX)] * 2, buf(4, CHUNKS, 2, 8, 128),
            buf(3, 5, 8, 128), *[buf(16, 128), buf(32, 128)] * 2, buf(3, 40, 128), buf(128, 128), buf(128, 128),
            *[buf(5, 24, 256)] * 2, *[buf(5, 24, 128)] * 4, buf(2, 2, 5, 8, 128), buf(2, 5, 8, 256),
            buf(2, 8, 128), buf(3, SECS, 2, 8, 128), buf(14, 32, 128), buf(5, 8, 128), buf(2, 15, 40, 128),
            buf(8, 128), buf(SLABS, 8, 128), buf(16, 128), buf(SECS, 16, 128), buf(16, 128), buf(SLABS, 16, 128),
            *[buf(4, CHUNKS, 21, 32, 128)] * 2, half(256, 3 * NX),
            *[buf(480, 3 * NX)] * 2, *[half(480, 6 * NX)] * 2, buf(480, 256), buf(1920, 128),
            buf(40, 128), buf(3, SECS, 40, 128), buf(8, 128), buf(SLABS, 8, 128),
            dma(10), dma(len(TABLES)), dma(18), dma(18), *[dma(3, SECS)] * 4, dma(SECS), dma(SECS), dma(6),
        ],
        compiler_params=pltpu.CompilerParams(
            collective_id=0, has_side_effects=True, vmem_limit_bytes=VMEM_LIMIT
        ),
        name="mega",
    )(
        jnp.transpose(moving_image, (1, 0, 2)),
        jnp.transpose(fixed_image, (1, 0, 2)),
        jnp.transpose(lattice_fine, (0, 2, 1, 3)),
        jnp.transpose(lattice_mid, (0, 3, 2, 1)),
        jnp.transpose(lattice_coarse, (0, 3, 2, 1)),
        offset_fine,
        jnp.transpose(offset_mid, (1, 2, 0)),
        jnp.transpose(offset_coarse, (0, 2, 1)),
        *(t[n] for n in TABLES),
    )
    fine, mid, coarse = pl.pallas_call(
        finish,
        out_shape=[shape(3, 5, 4, 33), shape(3, 9, 2, 33), shape(3, 3, 1, 9)],
        in_specs=[vmem],
        out_specs=[vmem] * 3,
        name="finish",
    )(result)
    return (
        jnp.transpose(fine, (0, 2, 1, 3)),
        jnp.transpose(mid, (0, 3, 2, 1)),
        jnp.transpose(coarse, (0, 3, 2, 1)),
    )


def solution(mesh):
    placed = (
        P("slab", "sec", None),
        P("slab", "sec", None),
        P(None, "slab", None, None),
        P(),
        P(),
        P(None, "slab", None),
        P(None, "slab", None),
        P(),
    )
    return jax.shard_map(
        body,
        mesh=mesh,
        in_specs=placed,
        out_specs=(P(None, "slab", None, None), P(), P()),
        check_vma=False,
    )
```

profile of v0, /device:TPU:1, one launch (start us, length us, event | category | flops | bytes accessed | tf_op | source)
XLA Modules:
  0.0 76.9 jit_solution(5297095501129427560)
XLA Ops:
  0.6 74.7 %mega.1.result = f32[264,128]{1,0:T(8,128)} custom-call(f32[20,80,640]{2,1,0:T(8,128)} %bitcast.10, f32[20,80,640]{2,1,0:T(8,128)} %bitcast.11, f32[3,5,4,33]{3,2,1,0:T(4,128)} %bitcast.12, f32[3,9,2,33]{3,2,1,0:T(2,128)} %bitcast.13, f32[3,3,1,9]{3,2,1,0:T(1,128)} %bitcast.14, s32[3,4,4]{2,1,0:T(4,128)} %off_fine.1, s32[1,1,3]{2,1,0:T(1,128)} %bitcast.16, ...), custom_call_target="tpu_custom_call" | custom-call | tf_op jit(solution)/shard_map/mega/pallas_call | solution.py:879
  75.3 1.6 %finish.1 = (f32[3,5,4,33]{3,2,1,0:T(4,128)}, f32[3,9,2,33]{3,2,1,0:T(2,128)}, f32[3,3,1,9]{3,2,1,0:T(1,128)}) custom-call(f32[264,128]{1,0:T(8,128)} %mega.1.result), custom_call_target="tpu_custom_call" | custom-call | tf_op jit(solution)/shard_map/finish/pallas_call | solution.py:912
where the time goes:
time: 77.1 us; the launch traced here: 76.9 us
  Pallas kernels  76.2 us (99%)
    pallas_call x1, Pallas kernels, body(): pl.pallas_call(kernel, out_shape=shape(264, 128), in_specs=[hbm, hbm, vme...  74.7 us
    pallas_call x1, Pallas kernels, body(): pl.pallas_call(finish, out_shape=[shape(3, 5, 4, 33), shape(3, 9, 2, 33),...  1.56 us

commit v1 on v0

--- a/solution.py
+++ b/solution.py
@@ -58,24 +58,25 @@
 @functools.cache
 def tables():
     t = {}
-    rz, ry = np.zeros((4, 4, 24, 64)), np.zeros((4, NY, 64))
+    rz, ry = np.zeros((4, 4, 20, 64)), np.zeros((4, NY, 64))
     z, y, x = np.arange(NZ), np.arange(NY), np.arange(NX)
     for r in range(4):
         for block in range(4):
             rows = z[20 * block : 20 * block + 20]
             for a in range(7):
-                rz[r, block, :20, a:40:8] = basis(rows, [a - 1], 1, 1)
+                rz[r, block, :, a:40:8] = basis(rows, [a - 1], 1, 1)
             for a in range(5):
-                rz[r, block, :20, 40 + a : 56 : 8] = basis(rows, [a - 2], 1, 4)
-                rz[r, block, :20, 56 + a : 57 + a] = basis(rows + 80 * r, [a - 2], 1, 16)
+                rz[r, block, :, 40 + a : 56 : 8] = basis(rows, [a - 2], 1, 4)
+                rz[r, block, :, 56 + a : 57 + a] = basis(rows + 80 * r, [a - 2], 1, 16)
     for s in range(4):
         for a in range(7):
             ry[s, :, a:40:8] = basis(y + 20 * s, range(5), 1, 1)
         for a in range(5):
             ry[s, :, 40 + a : 56 : 8] = basis(y + 20 * s, range(2), 1, 4)
             ry[s, :, 56 + a : 57 + a] = basis(y + 20 * s, [0], 1, 16)
+    rz = rz.reshape(4, 2, 40, 64)
     whole = rz[:, None, :, None] * ry[None, :, None, :, None, :]
-    high, low = two_parts(whole.reshape(16, 1920, 64))
+    high, low = two_parts(whole.reshape(16, 1600, 64))
     t["spread"] = np.concatenate([high, low, high, low], axis=2)
     t["gather"] = np.concatenate([high[:4, :, :40], low[:4, :, :40]], axis=2).transpose(0, 2, 1)
     across = np.zeros((3, 128, NX))
@@ -356,7 +357,7 @@
     ]
     load_fixed = [
         pltpu.make_async_copy(
-            fixed.at[:, :, pl.ds(128 * c, 128)], fx.at[c, :, pl.ds(0, NZ)], load_sem.at[CHUNKS + c]
+            fixed.at[:, :, pl.ds(128 * c, 128)], fx.at[c], load_sem.at[CHUNKS + c]
         )
         for c in range(CHUNKS)
     ]
@@ -431,10 +432,6 @@
     for c in range(CHUNKS):
         pad[c, :, 0:8, :] = jnp.zeros((28, 8, 128), F32)
         pad[c, :, 88:96, :] = jnp.zeros((28, 8, 128), F32)
-        fx[c, :, 80:88, :] = jnp.zeros((NY, 8, 128), F32)
-        for block in range(4):
-            at[block, c, :, 24:32, :] = jnp.zeros((21, 8, 128), F32)
-            by[block, c, :, 24:32, :] = jnp.zeros((21, 8, 128), F32)
     all_here()
     start_y_halos(0, 1)
     for c in range(CHUNKS):
@@ -472,7 +469,7 @@
 
         @pl.loop(0, 5, unroll=5)
         def _(group):
-            four = [fx[c, 4 * group + i, 0:80, :] for i in range(4)]
+            four = [fx[c, 4 * group + i] for i in range(4)]
             sums[group, :, lanes] = (four[0] + four[1]) + (four[2] + four[3])
 
     pooled_f[...] = pooled()
@@ -638,8 +635,8 @@
         window = [pad[c, 4 + oy + y, pl.ds(20 * block + 8 + oz, 24), :] for c in range(CHUNKS)]
         here, there = shift_lanes(window, ox), shift_lanes(window, ox + 1)
         for c in range(CHUNKS):
-            at[block, c, y, 0:24, :] = here[c]
-            by[block, c, y, 0:24, :] = there[c] - here[c]
+            at[block, c, y, 8:32, :] = here[c]
+            by[block, c, y, 8:32, :] = there[c] - here[c]
 
     def make_windows(blocks, ranges):
         @pl.loop(*blocks)
@@ -772,13 +769,24 @@
     columns[64:128, :] = upper
     columns[128:192, :] = lower
     columns[192:256, :] = lower
-    field_a[...] = dot(spread[0:480, :], columns[...])
-
-    rows_z = (pl.ds(0, 24), pl.ds(jnp.minimum(k + 1, 1), 24))
-
-    def fine_block(block, split, split_before, field, field_after):
+    field_a[...] = dot(spread[0:400, :], columns[...])
+
+    first_rows = lax.broadcasted_iota(jnp.int32, (8, 128), 0) < 4
+    steps_z = (jnp.minimum(k, 0), jnp.minimum(k + 1, 1))
+
+    def planes(ref, pair, c, y, z):
+        a, b = 2 * pair, 2 * pair + 1
+        middle = jnp.where(
+            first_rows, ref[a, c, y, pl.ds(24 + z, 8), :], ref[b, c, y, pl.ds(4 + z, 8), :]
+        )
+        return jnp.concatenate(
+            [ref[a, c, y, pl.ds(8 + z, 16), :], middle, ref[b, c, y, pl.ds(12 + z, 16), :]], axis=0
+        )
+
+    def fine_stage(stage, split, split_before, field, field_after):
         adjoint[...] = jnp.zeros_like(adjoint)
-        after = pl.ds(pl.multiple_of(480 * jnp.minimum(block + 1, 3), 480), 480)
+        pair, y_first = stage >> 1, 10 * (stage & 1)
+        after = pl.ds(pl.multiple_of(400 * jnp.minimum(stage + 1, 3), 400), 400)
 
         @pl.loop(0, 5)
         def _(i):
@@ -786,36 +794,35 @@
             field_after[:, lanes] = dot(spread[after, :], columns[:, lanes])
             lanes = pl.ds(pl.multiple_of(768 * i, 768), 768)
             adjoint[...] += dot(split_before[:, lanes], bx[lanes, :])
-            for pair in range(2):
-                for c in range(CHUNKS):
-                    found = []
-                    for h in range(2):
-                        y = 4 * i + 2 * pair + h
-                        corner = [[at[block, c, y + e, z, :] for e in (0, 1)] for z in rows_z]
-                        step = [[by[block, c, y + e, z, :] for e in (0, 1)] for z in rows_z]
-                        rows = pl.ds(pl.multiple_of(24 * y, 8), 24)
-                        fractions = [
-                            fraction(field[rows, NX * d + 128 * c : NX * d + 128 * c + 128]) for d in range(3)
-                        ]
-                        atlas = fx[c, y, pl.ds(20 * block, 24), :]
-                        found.append(weights(atlas, corner, step, fractions))
-                    rows = pl.ds(pl.multiple_of(96 * i + 48 * pair, 48), 48)
-                    for d in range(3):
-                        upper, lower = parts(jnp.concatenate([found[0][d], found[1][d]], axis=0))
-                        lane = 2 * NX * d + 128 * c
-                        split[rows, lane : lane + 128] = upper
-                        split[rows, lane + NX : lane + NX + 128] = lower
-
-        before = pl.ds(pl.multiple_of(480 * jnp.maximum(block - 1, 0), 480), 480)
+            for c in range(CHUNKS):
+                found = []
+                for h in range(2):
+                    y = y_first + 2 * i + h
+                    corner = [[planes(at, pair, c, y + e, z) for e in (0, 1)] for z in steps_z]
+                    step = [[planes(by, pair, c, y + e, z) for e in (0, 1)] for z in steps_z]
+                    rows = pl.ds(pl.multiple_of(80 * i + 40 * h, 8), 40)
+                    fractions = [
+                        fraction(field[rows, NX * d + 128 * c : NX * d + 128 * c + 128]) for d in range(3)
+                    ]
+                    atlas = fx[c, y, pl.ds(pl.multiple_of(40 * pair, 8), 40), :]
+                    found.append(weights(atlas, corner, step, fractions))
+                rows = pl.ds(pl.multiple_of(80 * i, 80), 80)
+                for d in range(3):
+                    upper, lower = parts(jnp.concatenate([found[0][d], found[1][d]], axis=0))
+                    lane = 2 * NX * d + 128 * c
+                    split[rows, lane : lane + 128] = upper
+                    split[rows, lane + NX : lane + NX + 128] = lower
+
+        before = pl.ds(pl.multiple_of(400 * jnp.maximum(stage - 1, 0), 400), 400)
         mixed[before, :] = adjoint[:, 0:128] + adjoint[:, 128:256]
 
     @pl.loop(0, 2)
     def _(two):
-        fine_block(2 * two, split_a, split_b, field_a, field_b)
-        fine_block(2 * two + 1, split_b, split_a, field_b, field_a)
+        fine_stage(2 * two, split_a, split_b, field_a, field_b)
+        fine_stage(2 * two + 1, split_b, split_a, field_b, field_a)
 
     wide = dot(split_b[...], bx[...])
-    mixed[1440:1920, :] = wide[:, 0:128] + wide[:, 128:256]
+    mixed[1200:1600, :] = wide[:, 0:128] + wide[:, 128:256]
     f_part[...] = dot_gather(gather[...], mixed[...])
     around(k, s, f_part, f_parts, fsend, frecv, "start")
     f_parts[1, s] = f_part[...]
@@ -883,14 +890,14 @@
         out_specs=vmem,
         scratch_shapes=[
             *[pltpu.VMEM(t[n].shape[which is not None :], t[n].dtype) for n, which in TABLES.items()],
-            buf(CHUNKS, 28, 96, 128), buf(CHUNKS, NY, 88, 128), buf(5, NZ, NX),
+            buf(CHUNKS, 28, 96, 128), buf(CHUNKS, NY, NZ, 128), buf(5, NZ, NX),
             *[buf(CHUNKS, 10, 8, 128)] * 4, *[buf(4, NZ, NX)] * 2, buf(4, CHUNKS, 2, 8, 128),
             buf(3, 5, 8, 128), *[buf(16, 128), buf(32, 128)] * 2, buf(3, 40, 128), buf(128, 128), buf(128, 128),
             *[buf(5, 24, 256)] * 2, *[buf(5, 24, 128)] * 4, buf(2, 2, 5, 8, 128), buf(2, 5, 8, 256),
             buf(2, 8, 128), buf(3, SECS, 2, 8, 128), buf(14, 32, 128), buf(5, 8, 128), buf(2, 15, 40, 128),
             buf(8, 128), buf(SLABS, 8, 128), buf(16, 128), buf(SECS, 16, 128), buf(16, 128), buf(SLABS, 16, 128),
-            *[buf(4, CHUNKS, 21, 32, 128)] * 2, half(256, 3 * NX),
-            *[buf(480, 3 * NX)] * 2, *[half(480, 6 * NX)] * 2, buf(480, 256), buf(1920, 128),
+            *[buf(4, CHUNKS, 21, 40, 128)] * 2, half(256, 3 * NX),
+            *[buf(400, 3 * NX)] * 2, *[half(400, 6 * NX)] * 2, buf(400, 256), buf(1600, 128),
             buf(40, 128), buf(3, SECS, 40, 128), buf(8, 128), buf(SLABS, 8, 128),
             dma(10), dma(len(TABLES)), dma(18), dma(18), *[dma(3, SECS)] * 4, dma(SECS), dma(SECS), dma(6),
         ],

time: 77.1 us -> 74.9 us (0.971)
  Pallas kernels: 76.2 us -> 74.1 us
    pallas_call x1, Pallas kernels: 74.7 us -> 72.5 us  [body(): pl.pallas_call(kernel, out_shape=shape(264, 128), in_specs=[hbm, hbm, vme...]
where the time goes in v1:
time: 74.9 us; the launch traced here: 74.7 us
  Pallas kernels  74.1 us (99%)
    pallas_call x1, Pallas kernels, body(): pl.pallas_call(kernel, out_shape=shape(264, 128), in_specs=[hbm, hbm, vme...  72.5 us
    pallas_call x1, Pallas kernels, body(): pl.pallas_call(finish, out_shape=[shape(3, 5, 4, 33), shape(3, 9, 2, 33),...  1.56 us

profile of v1, /device:TPU:1, one launch (start us, length us, event | category | flops | bytes accessed | tf_op | source)
XLA Modules:
  0.0 74.7 jit_solution(8799567213742944297)
XLA Ops:
  0.6 72.5 %mega.1.result = f32[264,128]{1,0:T(8,128)} custom-call(f32[20,80,640]{2,1,0:T(8,128)} %bitcast.10, f32[20,80,640]{2,1,0:T(8,128)} %bitcast.11, f32[3,5,4,33]{3,2,1,0:T(4,128)} %bitcast.12, f32[3,9,2,33]{3,2,1,0:T(2,128)} %bitcast.13, f32[3,3,1,9]{3,2,1,0:T(1,128)} %bitcast.14, s32[3,4,4]{2,1,0:T(4,128)} %off_fine.1, s32[1,1,3]{2,1,0:T(1,128)} %bitcast.16, ...), custom_call_target="tpu_custom_call" | custom-call | tf_op jit(solution)/shard_map/mega/pallas_call | solution.py:886
  73.1 1.6 %finish.1 = (f32[3,5,4,33]{3,2,1,0:T(4,128)}, f32[3,9,2,33]{3,2,1,0:T(2,128)}, f32[3,3,1,9]{3,2,1,0:T(1,128)}) custom-call(f32[264,128]{1,0:T(8,128)} %mega.1.result), custom_call_target="tpu_custom_call" | custom-call | tf_op jit(solution)/shard_map/finish/pallas_call | solution.py:919

commit v2 on v1

--- a/solution.py
+++ b/solution.py
@@ -497,6 +497,7 @@
     start(*mid_same)
     start_if(up, *mid_up)
     start_if(down, *mid_down)
+    start_y_halos(2)
 
     for ref in (lf_own, mt, ct, cv, mm):
         ref[...] = jnp.zeros_like(ref)
@@ -564,7 +565,7 @@
     c_tile[...] = dot_gather(cgather[...], total)[0:8]
     broadcast_start(k, s, c_tile, c_buf, bsem.at[0], bsem.at[1])
     c_buf[k] = c_tile[...]
-    start_y_halos(2, 3)
+    start_y_halos(3, 4)
     start(z_to_prev)
 
     mbt, mspread, mbx, mgather = table("mbt"), table("mspread"), table("mbx"), table("mgather")
@@ -674,7 +675,6 @@
             getattr(remote(m_part, m_parts.at[slot], tsend.at[other], trecv.at[slot], (k, other)), act)()
 
     part_copies("start")
-    start_y_halos(4)
     start_if(up, *corner_up)
     start_if(down, *corner_down)
     m_parts[s] = m_part[...]
@@ -717,21 +717,6 @@
     for copy in (z_to_next, z_to_prev):
         copy.wait_recv()
 
-    @pl.when(s > 0)
-    def _():
-        for copy in (to_bef, *corner_up):
-            copy.wait_recv()
-
-    @pl.when(s < SECS - 1)
-    def _():
-        for copy in (to_aft, *corner_down):
-            copy.wait_recv()
-
-    for c in range(CHUNKS):
-        lanes = slice(128 * c, 128 * c + 128)
-        pad[c, 0:4, 8:88, :] = y_bef[:, :, lanes]
-        pad[c, 24:28, 8:88, :] = y_aft[:, :, lanes]
-
     @pl.loop(0, NY // 2, unroll=2)
     def _(pair):
         for half in range(2):
@@ -740,6 +725,23 @@
                 pad[c, 2 * pair + half + 4, 4:8, :] = z_bef[c, pair, rows, :] * has_prev
                 pad[c, 2 * pair + half + 4, 88:92, :] = z_aft[c, pair, rows, :] * has_next
 
+    make_windows((0, 1), ((4, 16, 3),))
+    make_windows((3, 4), ((4, 16, 3),))
+
+    @pl.when(s > 0)
+    def _():
+        for copy in (to_bef, *corner_up):
+            copy.wait_recv()
+
+    @pl.when(s < SECS - 1)
+    def _():
+        for copy in (to_aft, *corner_down):
+            copy.wait_recv()
+
+    for c in range(CHUNKS):
+        lanes = slice(128 * c, 128 * c + 128)
+        pad[c, 0:4, 8:88, :] = y_bef[:, :, lanes]
+        pad[c, 24:28, 8:88, :] = y_aft[:, :, lanes]
     for y in range(4):
         rows = slice(4 * (y % 2), 4 * (y % 2) + 4)
         for c in range(CHUNKS):
@@ -749,9 +751,7 @@
                 pad[c, y, where, :] = corners[n, c, y // 2, rows, :] * keep
                 pad[c, 24 + y, where, :] = corners[2 + n, c, y // 2, rows, :] * keep
 
-    make_windows((1, 3), ((0, 4, 2), (16, 21, 5)))
-    make_windows((0, 1), ((0, 21, 3),))
-    make_windows((3, 4), ((0, 21, 3),))
+    make_windows((0, 4), ((0, 4, 2), (16, 21, 5)))
 
     spread, gather, bx, sum_m = table("spread"), table("gather"), table("bx"), table("sum_m")
 

time: 74.9 us -> 75.4 us (level)
  no operation moved by 1% of the time
where the time goes in v2:
time: 75.4 us; the launch traced here: 75.2 us
  Pallas kernels  74.5 us (99%)
    pallas_call x1, Pallas kernels, body(): pl.pallas_call(kernel, out_shape=shape(264, 128), in_specs=[hbm, hbm, vme...  73 us
    pallas_call x1, Pallas kernels, body(): pl.pallas_call(finish, out_shape=[shape(3, 5, 4, 33), shape(3, 9, 2, 33),...  1.56 us

profile of v2, /device:TPU:1, one launch (start us, length us, event | category | flops | bytes accessed | tf_op | source)
XLA Modules:
  0.0 75.2 jit_solution(11203628328583205508)
XLA Ops:
  0.6 73.0 %mega.1.result = f32[264,128]{1,0:T(8,128)} custom-call(f32[20,80,640]{2,1,0:T(8,128)} %bitcast.10, f32[20,80,640]{2,1,0:T(8,128)} %bitcast.11, f32[3,5,4,33]{3,2,1,0:T(4,128)} %bitcast.12, f32[3,9,2,33]{3,2,1,0:T(2,128)} %bitcast.13, f32[3,3,1,9]{3,2,1,0:T(1,128)} %bitcast.14, s32[3,4,4]{2,1,0:T(4,128)} %off_fine.1, s32[1,1,3]{2,1,0:T(1,128)} %bitcast.16, ...), custom_call_target="tpu_custom_call" | custom-call | tf_op jit(solution)/shard_map/mega/pallas_call | solution.py:886
  73.6 1.6 %finish.1 = (f32[3,5,4,33]{3,2,1,0:T(4,128)}, f32[3,9,2,33]{3,2,1,0:T(2,128)}, f32[3,3,1,9]{3,2,1,0:T(1,128)}) custom-call(f32[264,128]{1,0:T(8,128)} %mega.1.result), custom_call_target="tpu_custom_call" | custom-call | tf_op jit(solution)/shard_map/finish/pallas_call | solution.py:919
